TPU v7x, 32 devices: a whole 2x2x4 slice. The times are simulated.
32 devices in a mesh: gx: 8 (over z, core), gy: 4 (over y, x).
Axes of the slice: x: 2, y: 2, z: 4, core: 2. Of those that a mesh axis runs over, the one named last changes fastest.
Arguments:
- coil_sources: float32 [8, 128, 128, 128], P(None, 'gx', 'gy'), may hold values from -6 to 6
- tissue_labels: int32 [128, 128, 128], P('gx', 'gy'), may hold values from 0 to 5
- class_conductivity: float32 [6], replicated, may hold values from 0.1 to 2
Outputs:
- potential: float32 [8, 128, 128, 128], P(None, 'gx', 'gy')
All inputs are finite; a program needn't handle non-finite values.
Results may differ from a plain program's by a relative error of at most 0.0003.
Values sent between devices are 32-bit elements; how exact they have to be, the bound alone decides.
A program may use at most 192 MiB of HBM per device.

v0:
```python
import jax
import jax.numpy as jnp
from jax import lax
from jax.sharding import PartitionSpec as P

LEVELS = 5
SWEEPS = 2
COARSE_SWEEPS = 16
CLASSES = 6
damping = 0.8


def padded(cells, sides, width):
    for axis, dim in sides:
        count = lax.axis_size(axis)
        ends = count - 1
        head = lax.slice_in_dim(cells, 0, width, axis=dim)
        tail = lax.slice_in_dim(cells, cells.shape[dim] - width, cells.shape[dim], axis=dim)
        cells = jnp.concatenate(
            [
                lax.ppermute(tail, axis, [(i, (i + 1) % count) for i in range(ends)]),
                cells,
                lax.ppermute(head, axis, [((i + 1) % count, i) for i in range(ends)]),
            ],
            axis=dim,
        )
    return cells


def lookup_table(labels, table):
    result = jnp.zeros(labels.shape, jnp.float32)
    for klass in range(CLASSES):
        result = result + jnp.where(labels == klass, table[klass], jnp.float32(0.0))
    return result


def coarsen_cond(cond):
    sx, sy, sz = cond.shape
    return cond.reshape(sx // 2, 2, sy // 2, 2, sz // 2, 2).mean(axis=(1, 3, 5))


def restrict_sum(field):
    rr, sx, sy, sz = field.shape
    return field.reshape(rr, sx // 2, 2, sy // 2, 2, sz // 2, 2).sum(axis=(2, 4, 6))


def prolong_copy(field):
    rr, sx, sy, sz = field.shape
    grown = jnp.broadcast_to(field[:, :, None, :, None, :, None], (rr, sx, 2, sy, 2, sz, 2))
    return grown.reshape(rr, 2 * sx, 2 * sy, 2 * sz)


def face_coeffs(extended):
    centre = extended[1:-1, 1:-1, :]
    zpadded = jnp.pad(centre, ((0, 0), (0, 0), (1, 1)))
    others = [
        extended[2:, 1:-1, :],
        extended[:-2, 1:-1, :],
        extended[1:-1, 2:, :],
        extended[1:-1, :-2, :],
        zpadded[:, :, 2:],
        zpadded[:, :, :-2],
    ]
    coeffs = [
        jnp.where(other > 0, 2.0 * centre * other / (centre + other), centre) for other in others
    ]
    face_sum = coeffs[0] + coeffs[1] + coeffs[2] + coeffs[3] + coeffs[4] + coeffs[5]
    return (coeffs, face_sum)


def apply_operator(extended, field, coeffs, face_sum, scale):
    zpadded = jnp.pad(field, ((0, 0), (0, 0), (0, 0), (1, 1)))
    others = [
        extended[:, 2:, 1:-1, :],
        extended[:, :-2, 1:-1, :],
        extended[:, 1:-1, 2:, :],
        extended[:, 1:-1, :-2, :],
        zpadded[:, :, :, 2:],
        zpadded[:, :, :, :-2],
    ]
    total = coeffs[0] * others[0]
    for index in range(1, 6):
        total = total + coeffs[index] * others[index]
    return scale * (face_sum * field - total)


def field_rim(field):
    return padded(field, (("gx", 1), ("gy", 2)), 1)


def cond_rim(cond):
    return padded(cond, (("gx", 0), ("gy", 1)), 1)


def local_field_pad(field):
    return jnp.pad(field, ((0, 0), (1, 1), (1, 1), (0, 0)))


def local_cond_pad(cond):
    return jnp.pad(cond, ((1, 1), (1, 1), (0, 0)))


def relax(field, source, coeffs, face_sum, scale, count, padder):
    diagonal = scale * face_sum
    for sweep_index in range(count):
        field = (
            field
            + damping
            * (source - apply_operator(padder(field), field, coeffs, face_sum, scale))
            / diagonal
        )
    return field


def local_vcycle(level, source, conductivities, first):
    scale = jnp.float32(2.0**level)
    coeffs, face_sum = face_coeffs(local_cond_pad(conductivities[level - first]))
    diagonal = scale * face_sum
    field = damping * source / diagonal
    return relax(field, source, coeffs, face_sum, scale, COARSE_SWEEPS - 1, local_field_pad)


def local(coil_sources, tissue_labels, class_conductivity):
    depth = LEVELS - 1
    conductivities = [lookup_table(tissue_labels, class_conductivity)]
    for level in range(depth):
        conductivities.append(coarsen_cond(conductivities[-1]))
    stored = []
    source = coil_sources
    for level in range(depth):
        scale = jnp.float32(2.0**level)
        coeffs, face_sum = face_coeffs(cond_rim(conductivities[level]))
        field = damping * source / (scale * face_sum)
        field = relax(field, source, coeffs, face_sum, scale, SWEEPS - 1, field_rim)
        residual = source - apply_operator(field_rim(field), field, coeffs, face_sum, scale)
        stored.append((field, source, coeffs, face_sum, source, scale))
        source = restrict_sum(residual)
    block_x = source.shape[1]
    block_y = source.shape[2]
    gathered, coarse_cond = (
        lax.all_gather(source, "gy", axis=2, tiled=True),
        lax.all_gather(conductivities[depth], "gy", axis=1, tiled=True),
    )
    gathered, coarse_cond = (
        lax.all_gather(gathered, "gx", axis=1, tiled=True),
        lax.all_gather(coarse_cond, "gx", axis=0, tiled=True),
    )
    coarse_list = [coarse_cond]
    correction = local_vcycle(depth, gathered, coarse_list, depth)
    correction = lax.dynamic_slice_in_dim(correction, lax.axis_index("gx") * block_x, block_x, 1)
    correction = lax.dynamic_slice_in_dim(correction, lax.axis_index("gy") * block_y, block_y, 2)
    for level in range(depth - 1, -1, -1):
        field, source, coeffs, face_sum, source_ext, scale = stored[level]
        field = field + prolong_copy(correction)
        correction = relax(field, source, coeffs, face_sum, scale, SWEEPS, field_rim)
    return correction


def solution(mesh):
    in_specs = (P(None, "gx", "gy", None), P("gx", "gy", None), P())
    out_specs = P(None, "gx", "gy", None)
    return jax.shard_map(local, mesh=mesh, in_specs=in_specs, out_specs=out_specs, check_vma=False)
```

profile of v0, /device:TPU:16, one launch (start us, length us, event | category | flops | bytes accessed | tf_op | source)
XLA Modules:
  0.0 563.2 jit_solution(10171521428862776019)
XLA Ops:
  1.5 5.0 select_add_fusion
  12.1 18.1 %reshape.94 = f32[8,2,16,2,64,2]{5,4,3,2,1,0:T(8,128)} reshape(f32[16,32,128]{2,1,0:T(8,128)S(1)} %select_add_fusion) | data formatting | bytes 524288 | tf_op jit(solution)/shard_map/reshape | solution.py:39
  30.2 7.0 %reduce_sum.89 = f32[8,16,64]{2,1,0:T(8,128)S(1)} reduce(f32[8,2,16,2,64,2]{5,4,3,2,1,0:T(8,128)} %reshape.94, f32[]{:T(128)} %constant.32.clone.1), dimensions={1,3,5}, to_apply=%region_1.2 | reduce | flops 57344 | bytes 294916 | tf_op jit(solution)/shard_map/reduce_sum | solution.py:39
  50.3 4.5 collective-permute-start.3
  76.4 4.3 collective-permute-start.7
  83.4 6.3 %collective-permute-start.15 = (f32[10,1,64]{2,1,0:T(1,128)S(1)}, f32[10,1,64]{2,1,0:T(1,128)S(1)}, u32[]{:S(2)}, u32[]{:S(2)}) collective-permute-start(f32[10,1,64]{2,1,0:T(1,128)S(1)} %get-tuple-element.103), channel_id=1, source_target_pairs={{0,1},{1,2},{2,3},{4,5},{5,6},{6,7},{8,9},{9,10},{10,11},{12,13},{... | collective-permute-start | bytes 7688 | tf_op jit(solution)/shard_map/ppermute | solution.py:21
  90.0 4.6 fusion.7
  103.0 4.8 collective-permute-start.11
  114.2 4.4 fusion.13
  118.6 18.0 %copy.522 = f32[8,16,32,128]{0,3,2,1:T(8,128)} copy(f32[8,16,32,128]{3,2,1,0:T(8,128)} %fusion.13) | data formatting | bytes 4194304 | tf_op jit(solution)/shard_map/sub | solution.py:135
  136.6 24.3 %reduce_sum.88 = f32[8,8,16,64]{0,3,2,1:T(8,128)} reduce(f32[8,8,2,16,2,64,2]{0,6,5,4,3,2,1:T(2,128)} %bitcast.21, f32[]{:T(128)} %constant.32.clone.1), dimensions={2,4,6}, to_apply=%region_0.1 | reduce | flops 458752 | bytes 2359300 | tf_op jit(solution)/shard_map/reduce_sum | solution.py:44
  172.4 4.8 collective-permute-start.19
  180.6 5.2 collective-permute-start.27
  194.1 4.8 collective-permute-start.23
  208.1 4.8 reduce_sum.90
  231.9 5.2 collective-permute-start.39
  249.2 5.4 collective-permute-start.35
  274.1 7.1 %all-gather.4 = f32[4,2,8]{2,1,0:T(2,128)S(1)} all-gather(f32[1,2,8]{2,1,0:T(2,128)} %multiply_bitcast_fusion), channel_id=4, replica_groups=mesh['gx'=8,'gy'=4] {'gy'}, dimensions={0}, use_global_device_ids=true | all-gather | bytes 320 | tf_op jit(solution)/shard_map/all_gather | solution.py:142
  281.2 13.3 %all-gather.3 = f32[64,8]{1,0:T(8,128)S(1)} all-gather(f32[8,8]{1,0:T(8,128)S(1)} %bitcast.46), channel_id=5, replica_groups=mesh['gx'=8,'gy'=4] {'gx'}, dimensions={0}, use_global_device_ids=true | all-gather | bytes 2304 | tf_op jit(solution)/shard_map/all_gather | solution.py:146
  314.1 4.3 collective-permute-start.47
  328.6 7.7 %all-gather = f32[8,8,8]{2,0,1:T(8,128)S(1)} all-gather(f32[8,2,8]{2,0,1:T(8,128)} %copy.527), channel_id=2, replica_groups=mesh['gx'=8,'gy'=4] {'gy'}, dimensions={1}, use_global_device_ids=true | all-gather | bytes 2560 | tf_op jit(solution)/shard_map/all_gather | solution.py:141
  336.3 13.0 %all-gather.1 = f32[8,64,8]{2,0,1:T(8,128)S(1)} all-gather(f32[8,8,8]{2,0,1:T(8,128)S(1)} %all-gather), channel_id=3, replica_groups=mesh['gx'=8,'gy'=4] {'gx'}, dimensions={1}, use_global_device_ids=true | all-gather | bytes 18432 | tf_op jit(solution)/shard_map/all_gather | solution.py:145
  356.4 4.6 collective-permute-start.48
  370.8 4.2 collective-permute-done.50
  383.5 4.3 collective-permute-start.55
  408.3 4.3 collective-permute-done.58
  427.5 4.3 collective-permute-done.62
  454.5 4.2 collective-permute-done.66
  471.6 4.2 collective-permute-done.70
  480.8 16.0 %broadcast_in_dim.55 = f32[8,8,2,16,2,64,2]{0,6,5,4,3,2,1:T(2,128)} broadcast(f32[8,8,16,64]{0,3,2,1:T(8,128)} %copy.532), dimensions={0,1,3,5} | broadcast | bytes 2359296 | tf_op jit(solution)/shard_map/broadcast_in_dim | solution.py:49
  496.8 20.1 %copy.533 = f32[8,16,32,128]{3,2,1,0:T(8,128)} copy(f32[8,16,32,128]{0,3,2,1:T(8,128)} %bitcast.22) | data formatting | bytes 4194304 | tf_op jit(solution)/shard_map/reshape | solution.py:50
  558.5 4.5 fusion.31
  (451 shorter events, 312.7 us)
Async XLA Ops:
  6.5 42.4 %collective-permute-start.1 = (f32[1,32,128]{2,1,0:T(8,128)S(1)}, f32[1,32,128]{2,1,0:T(8,128)S(1)}, u32[]{:S(2)}, u32[]{:S(2)}) collective-permute-start(f32[1,32,128]{2,1,0:T(8,128)S(1)} %get-tuple-element.94), channel_id=1, source_target_pairs={{0,4},{4,8},{8,12},{12,16},{16,20},{20,24},{24,28},{1,5},{5,9},{9,... | collective-permute-start | bytes 49160 | tf_op jit(solution)/shard_map/ppermute | solution.py:21
  8.5 40.5 %collective-permute-start = (f32[1,32,128]{2,1,0:T(8,128)S(1)}, f32[1,32,128]{2,1,0:T(8,128)S(1)}, u32[]{:S(2)}, u32[]{:S(2)}) collective-permute-start(f32[1,32,128]{2,1,0:T(8,128)S(1)} %get-tuple-element.93), channel_id=1, source_target_pairs={{4,0},{8,4},{12,8},{16,12},{20,16},{24,20},{28,24},{5,1},{9,5},{13... | collective-permute-start | bytes 49160 | tf_op jit(solution)/shard_map/ppermute | solution.py:23
  37.9 42.8 %collective-permute-start.13 = (f32[1,16,64]{2,1,0:T(8,128)}, f32[1,16,64]{2,1,0:T(8,128)S(1)}, u32[]{:S(2)}, u32[]{:S(2)}) collective-permute-start(f32[1,16,64]{2,1,0:T(8,128)} %get-tuple-element.114), channel_id=1, source_target_pairs={{0,4},{4,8},{8,12},{12,16},{16,20},{20,24},{24,28},{1,5},{5,9},{9,... | collective-permute-start | bytes 12296 | tf_op jit(solution)/shard_map/ppermute | solution.py:21
  39.8 42.2 %collective-permute-start.12 = (f32[1,16,64]{2,1,0:T(8,128)}, f32[1,16,64]{2,1,0:T(8,128)S(1)}, u32[]{:S(2)}, u32[]{:S(2)}) collective-permute-start(f32[1,16,64]{2,1,0:T(8,128)} %get-tuple-element.113), channel_id=1, source_target_pairs={{4,0},{8,4},{12,8},{16,12},{20,16},{24,20},{28,24},{5,1},{9,5},{13... | collective-permute-start | bytes 12296 | tf_op jit(solution)/shard_map/ppermute | solution.py:23
  61.8 10.6 %collective-permute-start.4 = (f32[8,1,32,128]{3,2,1,0:T(8,128)}, f32[8,1,32,128]{3,2,1,0:T(8,128)}, u32[]{:S(2)}, u32[]{:S(2)}) collective-permute-start(f32[8,1,32,128]{3,2,1,0:T(8,128)} %get-tuple-element.58), channel_id=1, source_target_pairs={{4,0},{8,4},{12,8},{16,12},{20,16},{24,20},{28,24},{5,1},{9,5},{13... | collective-permute-start | bytes 393224 | tf_op jit(solution)/shard_map/ppermute | solution.py:23
  63.7 11.3 %collective-permute-start.5 = (f32[8,1,32,128]{3,2,1,0:T(8,128)}, f32[8,1,32,128]{3,2,1,0:T(8,128)}, u32[]{:S(2)}, u32[]{:S(2)}) collective-permute-start(f32[8,1,32,128]{3,2,1,0:T(8,128)} %get-tuple-element.57), channel_id=1, source_target_pairs={{0,4},{4,8},{8,12},{12,16},{16,20},{20,24},{24,28},{1,5},{5,9},{9,... | collective-permute-start | bytes 393224 | tf_op jit(solution)/shard_map/ppermute | solution.py:21
  66.7 111.8 %collective-permute-start.25 = (f32[1,8,32]{2,1,0:T(8,128)}, f32[1,8,32]{2,1,0:T(8,128)}, u32[]{:S(2)}, u32[]{:S(2)}) collective-permute-start(f32[1,8,32]{2,1,0:T(8,128)} %get-tuple-element.118), channel_id=1, source_target_pairs={{0,4},{4,8},{8,12},{12,16},{16,20},{20,24},{24,28},{1,5},{5,9},{9,... | collective-permute-start | bytes 3080 | tf_op jit(solution)/shard_map/ppermute | solution.py:21
  72.4 106.1 %collective-permute-start.24 = (f32[1,8,32]{2,1,0:T(8,128)}, f32[1,8,32]{2,1,0:T(8,128)}, u32[]{:S(2)}, u32[]{:S(2)}) collective-permute-start(f32[1,8,32]{2,1,0:T(8,128)} %get-tuple-element.117), channel_id=1, source_target_pairs={{4,0},{8,4},{12,8},{16,12},{20,16},{24,20},{28,24},{5,1},{9,5},{13... | collective-permute-start | bytes 3080 | tf_op jit(solution)/shard_map/ppermute | solution.py:23
  76.4 7.0 %collective-permute-start.7 = (f32[8,18,1,128]{3,0,2,1:T(8,128)S(1)}, f32[8,18,1,128]{3,0,2,1:T(8,128)S(1)}, u32[]{:S(2)}, u32[]{:S(2)}) collective-permute-start(f32[8,18,1,128]{3,0,2,1:T(8,128)S(1)} %copy.516), channel_id=1, source_target_pairs={{0,1},{1,2},{2,3},{4,5},{5,6},{6,7},{8,9},{9,10},{10,11},{12,13},{... | collective-permute-start | bytes 221192 | tf_op jit(solution)/shard_map/ppermute | solution.py:21
  80.7 9.1 %collective-permute-start.6 = (f32[8,18,1,128]{3,0,2,1:T(8,128)S(1)}, f32[8,18,1,128]{3,0,2,1:T(8,128)S(1)}, u32[]{:S(2)}, u32[]{:S(2)}) collective-permute-start(f32[8,18,1,128]{3,0,2,1:T(8,128)S(1)} %copy.514), channel_id=1, source_target_pairs={{1,0},{2,1},{3,2},{5,4},{6,5},{7,6},{9,8},{10,9},{11,10},{13,12},{... | collective-permute-start | bytes 221192 | tf_op jit(solution)/shard_map/ppermute | solution.py:23
  82.1 14.5 %collective-permute-start.14 = (f32[10,1,64]{2,1,0:T(1,128)S(1)}, f32[10,1,64]{2,1,0:T(1,128)S(1)}, u32[]{:S(2)}, u32[]{:S(2)}) collective-permute-start(f32[10,1,64]{2,1,0:T(1,128)S(1)} %get-tuple-element.104), channel_id=1, source_target_pairs={{1,0},{2,1},{3,2},{5,4},{6,5},{7,6},{9,8},{10,9},{11,10},{13,12},{... | collective-permute-start | bytes 7688 | tf_op jit(solution)/shard_map/ppermute | solution.py:23
  83.4 15.6 %collective-permute-start.15 = (f32[10,1,64]{2,1,0:T(1,128)S(1)}, f32[10,1,64]{2,1,0:T(1,128)S(1)}, u32[]{:S(2)}, u32[]{:S(2)}) collective-permute-start(f32[10,1,64]{2,1,0:T(1,128)S(1)} %get-tuple-element.103), channel_id=1, source_target_pairs={{0,1},{1,2},{2,3},{4,5},{5,6},{6,7},{8,9},{9,10},{10,11},{12,13},{... | collective-permute-start | bytes 7688 | tf_op jit(solution)/shard_map/ppermute | solution.py:21
  103.0 7.3 %collective-permute-start.11 = (f32[8,18,1,128]{3,0,2,1:T(8,128)S(1)}, f32[8,18,1,128]{3,0,2,1:T(8,128)S(1)}, u32[]{:S(2)}, u32[]{:S(2)}) collective-permute-start(f32[8,18,1,128]{3,0,2,1:T(8,128)S(1)} %copy.520), channel_id=1, source_target_pairs={{0,1},{1,2},{2,3},{4,5},{5,6},{6,7},{8,9},{9,10},{10,11},{12,13},{... | collective-permute-start | bytes 221192 | tf_op jit(solution)/shard_map/ppermute | solution.py:21
  172.4 13.4 %collective-permute-start.19 = (f32[8,10,1,64]{3,2,1,0:T(1,128)S(1)}, f32[8,10,1,64]{3,2,1,0:T(1,128)S(1)}, u32[]{:S(2)}, u32[]{:S(2)}) collective-permute-start(f32[8,10,1,64]{3,2,1,0:T(1,128)S(1)} %get-tuple-element.74), channel_id=1, source_target_pairs={{0,1},{1,2},{2,3},{4,5},{5,6},{6,7},{8,9},{9,10},{10,11},{12,13},{... | collective-permute-start | bytes 61448 | tf_op jit(solution)/shard_map/ppermute | solution.py:21
  177.2 8.6 %collective-permute-start.18 = (f32[8,10,1,64]{3,2,1,0:T(1,128)S(1)}, f32[8,10,1,64]{3,2,1,0:T(1,128)S(1)}, u32[]{:S(2)}, u32[]{:S(2)}) collective-permute-start(f32[8,10,1,64]{3,2,1,0:T(1,128)S(1)} %get-tuple-element.73), channel_id=1, source_target_pairs={{1,0},{2,1},{3,2},{5,4},{6,5},{7,6},{9,8},{10,9},{11,10},{13,12},{... | collective-permute-start | bytes 61448 | tf_op jit(solution)/shard_map/ppermute | solution.py:23
  179.3 11.6 %collective-permute-start.26 = (f32[6,1,32]{2,1,0:T(1,128)S(1)}, f32[6,1,32]{2,1,0:T(1,128)S(1)}, u32[]{:S(2)}, u32[]{:S(2)}) collective-permute-start(f32[6,1,32]{2,1,0:T(1,128)S(1)} %get-tuple-element.116), channel_id=1, source_target_pairs={{1,0},{2,1},{3,2},{5,4},{6,5},{7,6},{9,8},{10,9},{11,10},{13,12},{... | collective-permute-start | bytes 2312 | tf_op jit(solution)/shard_map/ppermute | solution.py:23
  180.6 10.3 %collective-permute-start.27 = (f32[6,1,32]{2,1,0:T(1,128)S(1)}, f32[6,1,32]{2,1,0:T(1,128)S(1)}, u32[]{:S(2)}, u32[]{:S(2)}) collective-permute-start(f32[6,1,32]{2,1,0:T(1,128)S(1)} %get-tuple-element.115), channel_id=1, source_target_pairs={{0,1},{1,2},{2,3},{4,5},{5,6},{6,7},{8,9},{9,10},{10,11},{12,13},{... | collective-permute-start | bytes 2312 | tf_op jit(solution)/shard_map/ppermute | solution.py:21
  194.1 6.7 %collective-permute-start.23 = (f32[8,10,1,64]{3,2,1,0:T(1,128)S(1)}, f32[8,10,1,64]{3,2,1,0:T(1,128)S(1)}, u32[]{:S(2)}, u32[]{:S(2)}) collective-permute-start(f32[8,10,1,64]{3,2,1,0:T(1,128)S(1)} %get-tuple-element.72), channel_id=1, source_target_pairs={{0,1},{1,2},{2,3},{4,5},{5,6},{6,7},{8,9},{9,10},{10,11},{12,13},{... | collective-permute-start | bytes 61448 | tf_op jit(solution)/shard_map/ppermute | solution.py:21
  214.8 10.6 %collective-permute-start.28 = (f32[8,1,8,32]{0,3,2,1:T(8,128)}, f32[8,1,8,32]{0,3,2,1:T(8,128)}, u32[]{:S(2)}, u32[]{:S(2)}) collective-permute-start(f32[8,1,8,32]{0,3,2,1:T(8,128)} %get-tuple-element.86), channel_id=1, source_target_pairs={{4,0},{8,4},{12,8},{16,12},{20,16},{24,20},{28,24},{5,1},{9,5},{13... | collective-permute-start | bytes 24584 | tf_op jit(solution)/shard_map/ppermute | solution.py:23
  216.7 8.7 %collective-permute-start.29 = (f32[8,1,8,32]{0,3,2,1:T(8,128)}, f32[8,1,8,32]{0,3,2,1:T(8,128)}, u32[]{:S(2)}, u32[]{:S(2)}) collective-permute-start(f32[8,1,8,32]{0,3,2,1:T(8,128)} %get-tuple-element.85), channel_id=1, source_target_pairs={{0,4},{4,8},{8,12},{12,16},{16,20},{20,24},{24,28},{1,5},{5,9},{9,... | collective-permute-start | bytes 24584 | tf_op jit(solution)/shard_map/ppermute | solution.py:21
  219.8 10.8 %collective-permute-start.37 = (f32[1,4,16]{2,1,0:T(4,128)}, f32[1,4,16]{2,1,0:T(4,128)S(1)}, u32[]{:S(2)}, u32[]{:S(2)}) collective-permute-start(f32[1,4,16]{2,1,0:T(4,128)} %get-tuple-element.123), channel_id=1, source_target_pairs={{0,4},{4,8},{8,12},{12,16},{16,20},{20,24},{24,28},{1,5},{5,9},{9,... | collective-permute-start | bytes 776 | tf_op jit(solution)/shard_map/ppermute | solution.py:21
  223.5 7.0 %collective-permute-start.36 = (f32[1,4,16]{2,1,0:T(4,128)}, f32[1,4,16]{2,1,0:T(4,128)S(1)}, u32[]{:S(2)}, u32[]{:S(2)}) collective-permute-start(f32[1,4,16]{2,1,0:T(4,128)} %get-tuple-element.122), channel_id=1, source_target_pairs={{4,0},{8,4},{12,8},{16,12},{20,16},{24,20},{28,24},{5,1},{9,5},{13... | collective-permute-start | bytes 776 | tf_op jit(solution)/shard_map/ppermute | solution.py:23
  226.4 10.7 %collective-permute-start.31 = (f32[8,6,1,32]{0,3,2,1:T(8,128)S(1)}, f32[8,6,1,32]{0,3,2,1:T(8,128)S(1)}, u32[]{:S(2)}, u32[]{:S(2)}) collective-permute-start(f32[8,6,1,32]{0,3,2,1:T(8,128)S(1)} %get-tuple-element.66), channel_id=1, source_target_pairs={{0,1},{1,2},{2,3},{4,5},{5,6},{6,7},{8,9},{9,10},{10,11},{12,13},{... | collective-permute-start | bytes 18440 | tf_op jit(solution)/shard_map/ppermute | solution.py:21
  229.2 7.9 %collective-permute-start.30 = (f32[8,6,1,32]{0,3,2,1:T(8,128)S(1)}, f32[8,6,1,32]{0,3,2,1:T(8,128)S(1)}, u32[]{:S(2)}, u32[]{:S(2)}) collective-permute-start(f32[8,6,1,32]{0,3,2,1:T(8,128)S(1)} %get-tuple-element.65), channel_id=1, source_target_pairs={{1,0},{2,1},{3,2},{5,4},{6,5},{7,6},{9,8},{10,9},{11,10},{13,12},{... | collective-permute-start | bytes 18440 | tf_op jit(solution)/shard_map/ppermute | solution.py:23
  230.6 14.0 %collective-permute-start.38 = (f32[4,1,16]{2,1,0:T(1,128)S(1)}, f32[4,1,16]{2,1,0:T(1,128)S(1)}, u32[]{:S(2)}, u32[]{:S(2)}) collective-permute-start(f32[4,1,16]{2,1,0:T(1,128)S(1)} %get-tuple-element.120), channel_id=1, source_target_pairs={{1,0},{2,1},{3,2},{5,4},{6,5},{7,6},{9,8},{10,9},{11,10},{13,12},{... | collective-permute-start | bytes 776 | tf_op jit(solution)/shard_map/ppermute | solution.py:23
  231.9 12.7 %collective-permute-start.39 = (f32[4,1,16]{2,1,0:T(1,128)S(1)}, f32[4,1,16]{2,1,0:T(1,128)S(1)}, u32[]{:S(2)}, u32[]{:S(2)}) collective-permute-start(f32[4,1,16]{2,1,0:T(1,128)S(1)} %get-tuple-element.119), channel_id=1, source_target_pairs={{0,1},{1,2},{2,3},{4,5},{5,6},{6,7},{8,9},{9,10},{10,11},{12,13},{... | collective-permute-start | bytes 776 | tf_op jit(solution)/shard_map/ppermute | solution.py:21
  249.2 10.3 %collective-permute-start.35 = (f32[8,6,1,32]{0,3,2,1:T(8,128)}, f32[8,6,1,32]{0,3,2,1:T(8,128)}, u32[]{:S(2)}, u32[]{:S(2)}) collective-permute-start(f32[8,6,1,32]{0,3,2,1:T(8,128)} %get-tuple-element.64), channel_id=1, source_target_pairs={{0,1},{1,2},{2,3},{4,5},{5,6},{6,7},{8,9},{9,10},{10,11},{12,13},{... | collective-permute-start | bytes 18440 | tf_op jit(solution)/shard_map/ppermute | solution.py:21
  254.6 7.2 %collective-permute-start.34 = (f32[8,6,1,32]{0,3,2,1:T(8,128)}, f32[8,6,1,32]{0,3,2,1:T(8,128)}, u32[]{:S(2)}, u32[]{:S(2)}) collective-permute-start(f32[8,6,1,32]{0,3,2,1:T(8,128)} %get-tuple-element.63), channel_id=1, source_target_pairs={{1,0},{2,1},{3,2},{5,4},{6,5},{7,6},{9,8},{10,9},{11,10},{13,12},{... | collective-permute-start | bytes 18440 | tf_op jit(solution)/shard_map/ppermute | solution.py:23
  268.5 25.9 %collective-permute-start.40 = (f32[8,1,4,16]{0,3,2,1:T(8,128)}, f32[8,1,4,16]{0,3,2,1:T(8,128)}, u32[]{:S(2)}, u32[]{:S(2)}) collective-permute-start(f32[8,1,4,16]{0,3,2,1:T(8,128)} %get-tuple-element.112), channel_id=1, source_target_pairs={{4,0},{8,4},{12,8},{16,12},{20,16},{24,20},{28,24},{5,1},{9,5},{13... | collective-permute-start | bytes 6152 | tf_op jit(solution)/shard_map/ppermute | solution.py:23
  270.4 24.0 %collective-permute-start.41 = (f32[8,1,4,16]{0,3,2,1:T(8,128)}, f32[8,1,4,16]{0,3,2,1:T(8,128)}, u32[]{:S(2)}, u32[]{:S(2)}) collective-permute-start(f32[8,1,4,16]{0,3,2,1:T(8,128)} %get-tuple-element.111), channel_id=1, source_target_pairs={{0,4},{4,8},{8,12},{12,16},{16,20},{20,24},{24,28},{1,5},{5,9},{9,... | collective-permute-start | bytes 6152 | tf_op jit(solution)/shard_map/ppermute | solution.py:21
  356.4 6.5 %collective-permute-start.48 = (f32[8,1,4,16]{0,3,2,1:T(8,128)S(1)}, f32[8,1,4,16]{0,3,2,1:T(8,128)S(1)}, u32[]{:S(2)}, u32[]{:S(2)}) collective-permute-start(f32[8,1,4,16]{0,3,2,1:T(8,128)S(1)} %get-tuple-element.108), channel_id=1, source_target_pairs={{4,0},{8,4},{12,8},{16,12},{20,16},{24,20},{28,24},{5,1},{9,5},{13... | collective-permute-start | bytes 6152 | tf_op jit(solution)/shard_map/ppermute | solution.py:23
  425.3 6.5 %collective-permute-start.62 = (f32[8,6,1,32]{0,3,2,1:T(8,128)S(1)}, f32[8,6,1,32]{0,3,2,1:T(8,128)S(1)}, u32[]{:S(2)}, u32[]{:S(2)}) collective-permute-start(f32[8,6,1,32]{0,3,2,1:T(8,128)S(1)} %get-tuple-element.59), channel_id=1, source_target_pairs={{1,0},{2,1},{3,2},{5,4},{6,5},{7,6},{9,8},{10,9},{11,10},{13,12},{... | collective-permute-start | bytes 18440 | tf_op jit(solution)/shard_map/ppermute | solution.py:23
  (139 other events, 2376.8 us)
where the time goes:
time: 574 us; the launch traced here: 563 us
  starting transfers between devices  202 us (35%)
  other arithmetic  116 us (20%)
  local copies, waits for them, and re-layouts  106 us (18%)
  waiting for transfers between devices  96.2 us (17%)
  blocking collectives  41.1 us (7%)
    ppermute x40, starting transfers between devices, padded(): lax.ppermute(tail, axis, [(i, (i + 1) % count) for i in range(ends)])  128 us
    ppermute x40, starting transfers between devices, padded(): lax.ppermute(head, axis, [((i + 1) % count, i) for i in range(ends)])  73.2 us
    ppermute x40, waiting for transfers between devices, padded(): lax.ppermute(head, axis, [((i + 1) % count, i) for i in range(ends)])  52.2 us
    ppermute x40, waiting for transfers between devices, padded(): lax.ppermute(tail, axis, [(i, (i + 1) % count) for i in range(ends)])  44.1 us
    reduce_sum x5, other arithmetic, restrict_sum(): field.reshape(rr, sx // 2, 2, sy // 2, 2, sz // 2, 2).sum(axis=(2, 4, 6))  33.5 us
    add x25, other arithmetic, relax(): field + damping * (source - apply_operator(padder(field), field, coeffs,...  30.3 us
    reshape x2, local copies, waits for them, and re-layouts, prolong_copy(): return grown.reshape(rr, 2 * sx, 2 * sy, 2 * sz)  23.7 us
    sub x2, local copies, waits for them, and re-layouts, local(): source - apply_operator(field_rim(field), field, coeffs, face_sum, scale)  20.7 us
  transfers between devices with their start and end apart: 80, of which 39 were waited for; matrix products, arithmetic and copies ran while one was open for 20% of the time, Pallas kernels for 0%

commit v1 on v0

--- a/solution.py
+++ b/solution.py
@@ -8,6 +8,19 @@
 COARSE_SWEEPS = 16
 CLASSES = 6
 damping = 0.8
+
+
+def collect(x, axis, dim):
+    ways = lax.axis_size(axis)
+    up = [(d, (d + 1) % ways) for d in range(ways)]
+    down = [(d, (d - 1) % ways) for d in range(ways)]
+    earlier, later = ([x], [x])
+    for _ in range(ways // 2):
+        earlier.append(lax.ppermute(earlier[-1], axis, up))
+    for _ in range((ways - 1) // 2):
+        later.append(lax.ppermute(later[-1], axis, down))
+    line = jnp.concatenate([*earlier[::-1], *later[1:]], axis=dim)
+    return jnp.roll(line, (lax.axis_index(axis) - ways // 2) * x.shape[dim], axis=dim)
 
 
 def padded(cells, sides, width):
@@ -142,7 +155,7 @@
         lax.all_gather(conductivities[depth], "gy", axis=1, tiled=True),
     )
     gathered, coarse_cond = (
-        lax.all_gather(gathered, "gx", axis=1, tiled=True),
+        collect(gathered, "gx", 1),
         lax.all_gather(coarse_cond, "gx", axis=0, tiled=True),
     )
     coarse_list = [coarse_cond]

time: 574 us -> 575 us (level)
  the two profiles are of different devices: /device:TPU:16 before, /device:TPU:8 now
where the time goes in v1:
time: 575 us; the launch traced here: 564 us
  starting transfers between devices  203 us (35%)
  other arithmetic  110 us (19%)
  local copies, waits for them, and re-layouts  109 us (19%)
  waiting for transfers between devices  108 us (19%)
  blocking collectives  30.6 us (5%)
    ppermute x40, starting transfers between devices, padded(): lax.ppermute(tail, axis, [(i, (i + 1) % count) for i in range(ends)])  127 us
    ppermute x40, starting transfers between devices, padded(): lax.ppermute(head, axis, [((i + 1) % count, i) for i in range(ends)])  71 us
    ppermute x40, waiting for transfers between devices, padded(): lax.ppermute(head, axis, [((i + 1) % count, i) for i in range(ends)])  52.7 us
    ppermute x40, waiting for transfers between devices, padded(): lax.ppermute(tail, axis, [(i, (i + 1) % count) for i in range(ends)])  50.8 us
    reduce_sum x5, other arithmetic, restrict_sum(): field.reshape(rr, sx // 2, 2, sy // 2, 2, sz // 2, 2).sum(axis=(2, 4, 6))  34.4 us
    add x25, other arithmetic, relax(): field + damping * (source - apply_operator(padder(field), field, coeffs,...  26.6 us
    reshape x2, local copies, waits for them, and re-layouts, prolong_copy(): return grown.reshape(rr, 2 * sx, 2 * sy, 2 * sz)  23.7 us
    broadcast_in_dim x5, local copies, waits for them, and re-layouts, prolong_copy(): jnp.broadcast_to(field[:, :, None, :, None, :, None], (rr, sx, 2, sy, 2,...  22.5 us
  transfers between devices with their start and end apart: 87, of which 47 were waited for; matrix products, arithmetic and copies ran while one was open for 20% of the time, Pallas kernels for 0%

profile of v1, /device:TPU:8, one launch (start us, length us, event | category | flops | bytes accessed | tf_op | source)
XLA Modules:
  0.0 563.8 jit_solution(11005918562014356223)
XLA Ops:
  1.5 4.7 select_add_fusion
  11.9 18.1 %reshape.94 = f32[8,2,16,2,64,2]{5,4,3,2,1,0:T(8,128)} reshape(f32[16,32,128]{2,1,0:T(8,128)S(1)} %select_add_fusion) | data formatting | bytes 524288 | tf_op jit(solution)/shard_map/reshape | solution.py:52
  30.0 7.0 %reduce_sum.89 = f32[8,16,64]{2,1,0:T(8,128)S(1)} reduce(f32[8,2,16,2,64,2]{5,4,3,2,1,0:T(8,128)} %reshape.94, f32[]{:T(128)} %constant.90.clone.1), dimensions={1,3,5}, to_apply=%region_1.2 | reduce | flops 57344 | bytes 294916 | tf_op jit(solution)/shard_map/reduce_sum | solution.py:52
  50.0 4.5 collective-permute-start.3
  76.1 4.3 collective-permute-start.7
  83.1 6.3 %collective-permute-start.15 = (f32[10,1,64]{2,1,0:T(1,128)S(1)}, f32[10,1,64]{2,1,0:T(1,128)S(1)}, u32[]{:S(2)}, u32[]{:S(2)}) collective-permute-start(f32[10,1,64]{2,1,0:T(1,128)S(1)} %get-tuple-element.103), channel_id=1, source_target_pairs={{0,1},{1,2},{2,3},{4,5},{5,6},{6,7},{8,9},{9,10},{10,11},{12,13},{... | collective-permute-start | bytes 7688 | tf_op jit(solution)/shard_map/ppermute | solution.py:34
  89.7 4.6 fusion.7
  102.7 4.8 collective-permute-start.11
  113.9 4.4 fusion.13
  118.3 18.0 %copy.522 = f32[8,16,32,128]{0,3,2,1:T(8,128)} copy(f32[8,16,32,128]{3,2,1,0:T(8,128)} %fusion.13) | data formatting | bytes 4194304 | tf_op jit(solution)/shard_map/sub | solution.py:148
  136.2 24.2 %reduce_sum.88 = f32[8,8,16,64]{0,3,2,1:T(8,128)} reduce(f32[8,8,2,16,2,64,2]{0,6,5,4,3,2,1:T(2,128)} %bitcast.23, f32[]{:T(128)} %constant.90.clone.1), dimensions={2,4,6}, to_apply=%region_0.1 | reduce | flops 458752 | bytes 2359300 | tf_op jit(solution)/shard_map/reduce_sum | solution.py:57
  172.0 4.8 collective-permute-start.19
  180.2 5.2 collective-permute-start.27
  193.8 4.8 collective-permute-start.23
  207.8 4.8 reduce_sum.90
  229.8 5.2 collective-permute-start.39
  244.9 4.8 collective-permute-start.35
  251.9 4.3 collective-permute-done.34
  272.9 4.2 collective-permute-done.42
  302.5 8.5 %all-gather = f32[8,8,8]{2,0,1:T(8,128)} all-gather(f32[8,2,8]{2,0,1:T(8,128)} %copy.527), channel_id=2, replica_groups=mesh['gx'=8,'gy'=4] {'gy'}, dimensions={1}, use_global_device_ids=true | all-gather | bytes 2560 | tf_op jit(solution)/shard_map/all_gather | solution.py:154
  312.4 7.3 %all-gather.3 = f32[4,2,8]{2,1,0:T(2,128)S(1)} all-gather(f32[1,2,8]{2,1,0:T(2,128)} %multiply_bitcast_fusion), channel_id=3, replica_groups=mesh['gx'=8,'gy'=4] {'gy'}, dimensions={0}, use_global_device_ids=true | all-gather | bytes 320 | tf_op jit(solution)/shard_map/all_gather | solution.py:155
  319.7 14.8 %all-gather.2 = f32[64,8]{1,0:T(8,128)S(1)} all-gather(f32[8,8]{1,0:T(8,128)S(1)} %bitcast.32), channel_id=4, replica_groups=mesh['gx'=8,'gy'=4] {'gx'}, dimensions={0}, use_global_device_ids=true | all-gather | bytes 2304 | tf_op jit(solution)/shard_map/all_gather | solution.py:159
  360.8 6.0 %collective-permute-done.56 = f32[8,1,4,16]{0,3,2,1:T(8,128)S(1)} collective-permute-done((f32[8,1,4,16]{0,3,2,1:T(8,128)S(1)}, f32[8,1,4,16]{0,3,2,1:T(8,128)S(1)}, u32[]{:S(2)}, u32[]{:S(2)}) %collective-permute-start.56) | collective-permute-done | bytes 2080 | tf_op jit(solution)/shard_map/ppermute | solution.py:34
  371.6 4.2 collective-permute-done.57
  384.3 4.3 collective-permute-start.62
  409.1 4.3 collective-permute-done.65
  428.3 4.3 collective-permute-done.69
  455.2 4.2 collective-permute-done.73
  472.2 4.2 collective-permute-done.77
  481.4 16.0 %broadcast_in_dim.55 = f32[8,8,2,16,2,64,2]{0,6,5,4,3,2,1:T(2,128)} broadcast(f32[8,8,16,64]{0,3,2,1:T(8,128)} %copy.532), dimensions={0,1,3,5} | broadcast | bytes 2359296 | tf_op jit(solution)/shard_map/broadcast_in_dim | solution.py:62
  497.4 20.1 %copy.533 = f32[8,16,32,128]{3,2,1,0:T(8,128)} copy(f32[8,16,32,128]{0,3,2,1:T(8,128)} %bitcast.24) | data formatting | bytes 4194304 | tf_op jit(solution)/shard_map/reshape | solution.py:63
  559.1 4.5 fusion.31
  (448 shorter events, 319.0 us)
Async XLA Ops:
  6.3 42.4 %collective-permute-start.1 = (f32[1,32,128]{2,1,0:T(8,128)S(1)}, f32[1,32,128]{2,1,0:T(8,128)S(1)}, u32[]{:S(2)}, u32[]{:S(2)}) collective-permute-start(f32[1,32,128]{2,1,0:T(8,128)S(1)} %get-tuple-element.94), channel_id=1, source_target_pairs={{0,4},{4,8},{8,12},{12,16},{16,20},{20,24},{24,28},{1,5},{5,9},{9,... | collective-permute-start | bytes 49160 | tf_op jit(solution)/shard_map/ppermute | solution.py:34
  8.2 40.5 %collective-permute-start = (f32[1,32,128]{2,1,0:T(8,128)S(1)}, f32[1,32,128]{2,1,0:T(8,128)S(1)}, u32[]{:S(2)}, u32[]{:S(2)}) collective-permute-start(f32[1,32,128]{2,1,0:T(8,128)S(1)} %get-tuple-element.93), channel_id=1, source_target_pairs={{4,0},{8,4},{12,8},{16,12},{20,16},{24,20},{28,24},{5,1},{9,5},{13... | collective-permute-start | bytes 49160 | tf_op jit(solution)/shard_map/ppermute | solution.py:36
  37.6 42.8 %collective-permute-start.13 = (f32[1,16,64]{2,1,0:T(8,128)}, f32[1,16,64]{2,1,0:T(8,128)S(1)}, u32[]{:S(2)}, u32[]{:S(2)}) collective-permute-start(f32[1,16,64]{2,1,0:T(8,128)} %get-tuple-element.114), channel_id=1, source_target_pairs={{0,4},{4,8},{8,12},{12,16},{16,20},{20,24},{24,28},{1,5},{5,9},{9,... | collective-permute-start | bytes 12296 | tf_op jit(solution)/shard_map/ppermute | solution.py:34
  39.6 42.2 %collective-permute-start.12 = (f32[1,16,64]{2,1,0:T(8,128)}, f32[1,16,64]{2,1,0:T(8,128)S(1)}, u32[]{:S(2)}, u32[]{:S(2)}) collective-permute-start(f32[1,16,64]{2,1,0:T(8,128)} %get-tuple-element.113), channel_id=1, source_target_pairs={{4,0},{8,4},{12,8},{16,12},{20,16},{24,20},{28,24},{5,1},{9,5},{13... | collective-permute-start | bytes 12296 | tf_op jit(solution)/shard_map/ppermute | solution.py:36
  61.5 10.6 %collective-permute-start.4 = (f32[8,1,32,128]{3,2,1,0:T(8,128)}, f32[8,1,32,128]{3,2,1,0:T(8,128)}, u32[]{:S(2)}, u32[]{:S(2)}) collective-permute-start(f32[8,1,32,128]{3,2,1,0:T(8,128)} %get-tuple-element.58), channel_id=1, source_target_pairs={{4,0},{8,4},{12,8},{16,12},{20,16},{24,20},{28,24},{5,1},{9,5},{13... | collective-permute-start | bytes 393224 | tf_op jit(solution)/shard_map/ppermute | solution.py:36
  63.4 11.3 %collective-permute-start.5 = (f32[8,1,32,128]{3,2,1,0:T(8,128)}, f32[8,1,32,128]{3,2,1,0:T(8,128)}, u32[]{:S(2)}, u32[]{:S(2)}) collective-permute-start(f32[8,1,32,128]{3,2,1,0:T(8,128)} %get-tuple-element.57), channel_id=1, source_target_pairs={{0,4},{4,8},{8,12},{12,16},{16,20},{20,24},{24,28},{1,5},{5,9},{9,... | collective-permute-start | bytes 393224 | tf_op jit(solution)/shard_map/ppermute | solution.py:34
  66.4 111.7 %collective-permute-start.25 = (f32[1,8,32]{2,1,0:T(8,128)}, f32[1,8,32]{2,1,0:T(8,128)}, u32[]{:S(2)}, u32[]{:S(2)}) collective-permute-start(f32[1,8,32]{2,1,0:T(8,128)} %get-tuple-element.118), channel_id=1, source_target_pairs={{0,4},{4,8},{8,12},{12,16},{16,20},{20,24},{24,28},{1,5},{5,9},{9,... | collective-permute-start | bytes 3080 | tf_op jit(solution)/shard_map/ppermute | solution.py:34
  72.1 106.1 %collective-permute-start.24 = (f32[1,8,32]{2,1,0:T(8,128)}, f32[1,8,32]{2,1,0:T(8,128)}, u32[]{:S(2)}, u32[]{:S(2)}) collective-permute-start(f32[1,8,32]{2,1,0:T(8,128)} %get-tuple-element.117), channel_id=1, source_target_pairs={{4,0},{8,4},{12,8},{16,12},{20,16},{24,20},{28,24},{5,1},{9,5},{13... | collective-permute-start | bytes 3080 | tf_op jit(solution)/shard_map/ppermute | solution.py:36
  76.1 7.0 %collective-permute-start.7 = (f32[8,18,1,128]{3,0,2,1:T(8,128)S(1)}, f32[8,18,1,128]{3,0,2,1:T(8,128)S(1)}, u32[]{:S(2)}, u32[]{:S(2)}) collective-permute-start(f32[8,18,1,128]{3,0,2,1:T(8,128)S(1)} %copy.516), channel_id=1, source_target_pairs={{0,1},{1,2},{2,3},{4,5},{5,6},{6,7},{8,9},{9,10},{10,11},{12,13},{... | collective-permute-start | bytes 221192 | tf_op jit(solution)/shard_map/ppermute | solution.py:34
  80.4 9.1 %collective-permute-start.6 = (f32[8,18,1,128]{3,0,2,1:T(8,128)S(1)}, f32[8,18,1,128]{3,0,2,1:T(8,128)S(1)}, u32[]{:S(2)}, u32[]{:S(2)}) collective-permute-start(f32[8,18,1,128]{3,0,2,1:T(8,128)S(1)} %copy.514), channel_id=1, source_target_pairs={{1,0},{2,1},{3,2},{5,4},{6,5},{7,6},{9,8},{10,9},{11,10},{13,12},{... | collective-permute-start | bytes 221192 | tf_op jit(solution)/shard_map/ppermute | solution.py:36
  81.8 14.5 %collective-permute-start.14 = (f32[10,1,64]{2,1,0:T(1,128)S(1)}, f32[10,1,64]{2,1,0:T(1,128)S(1)}, u32[]{:S(2)}, u32[]{:S(2)}) collective-permute-start(f32[10,1,64]{2,1,0:T(1,128)S(1)} %get-tuple-element.104), channel_id=1, source_target_pairs={{1,0},{2,1},{3,2},{5,4},{6,5},{7,6},{9,8},{10,9},{11,10},{13,12},{... | collective-permute-start | bytes 7688 | tf_op jit(solution)/shard_map/ppermute | solution.py:36
  83.1 15.6 %collective-permute-start.15 = (f32[10,1,64]{2,1,0:T(1,128)S(1)}, f32[10,1,64]{2,1,0:T(1,128)S(1)}, u32[]{:S(2)}, u32[]{:S(2)}) collective-permute-start(f32[10,1,64]{2,1,0:T(1,128)S(1)} %get-tuple-element.103), channel_id=1, source_target_pairs={{0,1},{1,2},{2,3},{4,5},{5,6},{6,7},{8,9},{9,10},{10,11},{12,13},{... | collective-permute-start | bytes 7688 | tf_op jit(solution)/shard_map/ppermute | solution.py:34
  102.7 7.3 %collective-permute-start.11 = (f32[8,18,1,128]{3,0,2,1:T(8,128)S(1)}, f32[8,18,1,128]{3,0,2,1:T(8,128)S(1)}, u32[]{:S(2)}, u32[]{:S(2)}) collective-permute-start(f32[8,18,1,128]{3,0,2,1:T(8,128)S(1)} %copy.520), channel_id=1, source_target_pairs={{0,1},{1,2},{2,3},{4,5},{5,6},{6,7},{8,9},{9,10},{10,11},{12,13},{... | collective-permute-start | bytes 221192 | tf_op jit(solution)/shard_map/ppermute | solution.py:34
  172.0 13.4 %collective-permute-start.19 = (f32[8,10,1,64]{3,2,1,0:T(1,128)S(1)}, f32[8,10,1,64]{3,2,1,0:T(1,128)S(1)}, u32[]{:S(2)}, u32[]{:S(2)}) collective-permute-start(f32[8,10,1,64]{3,2,1,0:T(1,128)S(1)} %get-tuple-element.74), channel_id=1, source_target_pairs={{0,1},{1,2},{2,3},{4,5},{5,6},{6,7},{8,9},{9,10},{10,11},{12,13},{... | collective-permute-start | bytes 61448 | tf_op jit(solution)/shard_map/ppermute | solution.py:34
  176.8 8.6 %collective-permute-start.18 = (f32[8,10,1,64]{3,2,1,0:T(1,128)S(1)}, f32[8,10,1,64]{3,2,1,0:T(1,128)S(1)}, u32[]{:S(2)}, u32[]{:S(2)}) collective-permute-start(f32[8,10,1,64]{3,2,1,0:T(1,128)S(1)} %get-tuple-element.73), channel_id=1, source_target_pairs={{1,0},{2,1},{3,2},{5,4},{6,5},{7,6},{9,8},{10,9},{11,10},{13,12},{... | collective-permute-start | bytes 61448 | tf_op jit(solution)/shard_map/ppermute | solution.py:36
  178.9 11.6 %collective-permute-start.26 = (f32[6,1,32]{2,1,0:T(1,128)S(1)}, f32[6,1,32]{2,1,0:T(1,128)S(1)}, u32[]{:S(2)}, u32[]{:S(2)}) collective-permute-start(f32[6,1,32]{2,1,0:T(1,128)S(1)} %get-tuple-element.116), channel_id=1, source_target_pairs={{1,0},{2,1},{3,2},{5,4},{6,5},{7,6},{9,8},{10,9},{11,10},{13,12},{... | collective-permute-start | bytes 2312 | tf_op jit(solution)/shard_map/ppermute | solution.py:36
  180.2 10.3 %collective-permute-start.27 = (f32[6,1,32]{2,1,0:T(1,128)S(1)}, f32[6,1,32]{2,1,0:T(1,128)S(1)}, u32[]{:S(2)}, u32[]{:S(2)}) collective-permute-start(f32[6,1,32]{2,1,0:T(1,128)S(1)} %get-tuple-element.115), channel_id=1, source_target_pairs={{0,1},{1,2},{2,3},{4,5},{5,6},{6,7},{8,9},{9,10},{10,11},{12,13},{... | collective-permute-start | bytes 2312 | tf_op jit(solution)/shard_map/ppermute | solution.py:34
  193.8 6.7 %collective-permute-start.23 = (f32[8,10,1,64]{3,2,1,0:T(1,128)S(1)}, f32[8,10,1,64]{3,2,1,0:T(1,128)S(1)}, u32[]{:S(2)}, u32[]{:S(2)}) collective-permute-start(f32[8,10,1,64]{3,2,1,0:T(1,128)S(1)} %get-tuple-element.72), channel_id=1, source_target_pairs={{0,1},{1,2},{2,3},{4,5},{5,6},{6,7},{8,9},{9,10},{10,11},{12,13},{... | collective-permute-start | bytes 61448 | tf_op jit(solution)/shard_map/ppermute | solution.py:34
  213.7 10.6 %collective-permute-start.28 = (f32[8,1,8,32]{0,3,2,1:T(8,128)S(1)}, f32[8,1,8,32]{0,3,2,1:T(8,128)S(1)}, u32[]{:S(2)}, u32[]{:S(2)}) collective-permute-start(f32[8,1,8,32]{0,3,2,1:T(8,128)S(1)} %get-tuple-element.86), channel_id=1, source_target_pairs={{4,0},{8,4},{12,8},{16,12},{20,16},{24,20},{28,24},{5,1},{9,5},{13... | collective-permute-start | bytes 24584 | tf_op jit(solution)/shard_map/ppermute | solution.py:36
  215.7 8.7 %collective-permute-start.29 = (f32[8,1,8,32]{0,3,2,1:T(8,128)S(1)}, f32[8,1,8,32]{0,3,2,1:T(8,128)S(1)}, u32[]{:S(2)}, u32[]{:S(2)}) collective-permute-start(f32[8,1,8,32]{0,3,2,1:T(8,128)S(1)} %get-tuple-element.85), channel_id=1, source_target_pairs={{0,4},{4,8},{8,12},{12,16},{16,20},{20,24},{24,28},{1,5},{5,9},{9,... | collective-permute-start | bytes 24584 | tf_op jit(solution)/shard_map/ppermute | solution.py:34
  218.8 9.7 %collective-permute-start.37 = (f32[1,4,16]{2,1,0:T(4,128)S(1)}, f32[1,4,16]{2,1,0:T(4,128)S(1)}, u32[]{:S(2)}, u32[]{:S(2)}) collective-permute-start(f32[1,4,16]{2,1,0:T(4,128)S(1)} %get-tuple-element.123), channel_id=1, source_target_pairs={{0,4},{4,8},{8,12},{12,16},{16,20},{20,24},{24,28},{1,5},{5,9},{9,... | collective-permute-start | bytes 776 | tf_op jit(solution)/shard_map/ppermute | solution.py:34
  221.9 6.7 %collective-permute-start.36 = (f32[1,4,16]{2,1,0:T(4,128)S(1)}, f32[1,4,16]{2,1,0:T(4,128)S(1)}, u32[]{:S(2)}, u32[]{:S(2)}) collective-permute-start(f32[1,4,16]{2,1,0:T(4,128)S(1)} %get-tuple-element.122), channel_id=1, source_target_pairs={{4,0},{8,4},{12,8},{16,12},{20,16},{24,20},{28,24},{5,1},{9,5},{13... | collective-permute-start | bytes 776 | tf_op jit(solution)/shard_map/ppermute | solution.py:36
  224.4 10.7 %collective-permute-start.31 = (f32[8,6,1,32]{0,3,2,1:T(8,128)S(1)}, f32[8,6,1,32]{0,3,2,1:T(8,128)S(1)}, u32[]{:S(2)}, u32[]{:S(2)}) collective-permute-start(f32[8,6,1,32]{0,3,2,1:T(8,128)S(1)} %get-tuple-element.66), channel_id=1, source_target_pairs={{0,1},{1,2},{2,3},{4,5},{5,6},{6,7},{8,9},{9,10},{10,11},{12,13},{... | collective-permute-start | bytes 18440 | tf_op jit(solution)/shard_map/ppermute | solution.py:34
  227.2 7.8 %collective-permute-start.30 = (f32[8,6,1,32]{0,3,2,1:T(8,128)S(1)}, f32[8,6,1,32]{0,3,2,1:T(8,128)S(1)}, u32[]{:S(2)}, u32[]{:S(2)}) collective-permute-start(f32[8,6,1,32]{0,3,2,1:T(8,128)S(1)} %get-tuple-element.65), channel_id=1, source_target_pairs={{1,0},{2,1},{3,2},{5,4},{6,5},{7,6},{9,8},{10,9},{11,10},{13,12},{... | collective-permute-start | bytes 18440 | tf_op jit(solution)/shard_map/ppermute | solution.py:36
  228.5 12.5 %collective-permute-start.38 = (f32[4,1,16]{2,1,0:T(1,128)S(1)}, f32[4,1,16]{2,1,0:T(1,128)S(1)}, u32[]{:S(2)}, u32[]{:S(2)}) collective-permute-start(f32[4,1,16]{2,1,0:T(1,128)S(1)} %get-tuple-element.120), channel_id=1, source_target_pairs={{1,0},{2,1},{3,2},{5,4},{6,5},{7,6},{9,8},{10,9},{11,10},{13,12},{... | collective-permute-start | bytes 776 | tf_op jit(solution)/shard_map/ppermute | solution.py:36
  229.8 11.2 %collective-permute-start.39 = (f32[4,1,16]{2,1,0:T(1,128)S(1)}, f32[4,1,16]{2,1,0:T(1,128)S(1)}, u32[]{:S(2)}, u32[]{:S(2)}) collective-permute-start(f32[4,1,16]{2,1,0:T(1,128)S(1)} %get-tuple-element.119), channel_id=1, source_target_pairs={{0,1},{1,2},{2,3},{4,5},{5,6},{6,7},{8,9},{9,10},{10,11},{12,13},{... | collective-permute-start | bytes 776 | tf_op jit(solution)/shard_map/ppermute | solution.py:34
  244.9 7.0 %collective-permute-start.35 = (f32[8,6,1,32]{0,3,2,1:T(8,128)S(1)}, f32[8,6,1,32]{0,3,2,1:T(8,128)S(1)}, u32[]{:S(2)}, u32[]{:S(2)}) collective-permute-start(f32[8,6,1,32]{0,3,2,1:T(8,128)S(1)} %get-tuple-element.64), channel_id=1, source_target_pairs={{0,1},{1,2},{2,3},{4,5},{5,6},{6,7},{8,9},{9,10},{10,11},{12,13},{... | collective-permute-start | bytes 18440 | tf_op jit(solution)/shard_map/ppermute | solution.py:34
  249.8 6.5 %collective-permute-start.34 = (f32[8,6,1,32]{0,3,2,1:T(8,128)S(1)}, f32[8,6,1,32]{0,3,2,1:T(8,128)S(1)}, u32[]{:S(2)}, u32[]{:S(2)}) collective-permute-start(f32[8,6,1,32]{0,3,2,1:T(8,128)S(1)} %get-tuple-element.63), channel_id=1, source_target_pairs={{1,0},{2,1},{3,2},{5,4},{6,5},{7,6},{9,8},{10,9},{11,10},{13,12},{... | collective-permute-start | bytes 18440 | tf_op jit(solution)/shard_map/ppermute | solution.py:36
  288.3 7.5 %collective-permute-start.47 = (f32[8,4,1,16]{0,3,2,1:T(8,128)}, f32[8,4,1,16]{0,3,2,1:T(8,128)}, u32[]{:S(2)}, u32[]{:S(2)}) collective-permute-start(f32[8,4,1,16]{0,3,2,1:T(8,128)} %get-tuple-element.100), channel_id=1, source_target_pairs={{0,1},{1,2},{2,3},{4,5},{5,6},{6,7},{8,9},{9,10},{10,11},{12,13},{... | collective-permute-start | bytes 6152 | tf_op jit(solution)/shard_map/ppermute | solution.py:34
  311.1 23.4 %collective-permute-start.48 = (f32[8,1,8,8]{3,0,2,1:T(8,128)}, f32[8,1,8,8]{3,0,2,1:T(8,128)}, u32[]{:S(2)}, u32[]{:S(2)}) collective-permute-start(f32[8,1,8,8]{3,0,2,1:T(8,128)} %bitcast.10), channel_id=1, source_target_pairs={{0,4},{4,8},{8,12},{12,16},{16,20},{20,24},{24,28},{28,0},{1,5},{5... | collective-permute-start | bytes 6152 | tf_op jit(solution)/shard_map/ppermute | solution.py:19
  358.9 7.9 %collective-permute-start.56 = (f32[8,1,4,16]{0,3,2,1:T(8,128)S(1)}, f32[8,1,4,16]{0,3,2,1:T(8,128)S(1)}, u32[]{:S(2)}, u32[]{:S(2)}) collective-permute-start(f32[8,1,4,16]{0,3,2,1:T(8,128)S(1)} %get-tuple-element.107), channel_id=1, source_target_pairs={{0,4},{4,8},{8,12},{12,16},{16,20},{20,24},{24,28},{1,5},{5,9},{9,... | collective-permute-start | bytes 6152 | tf_op jit(solution)/shard_map/ppermute | solution.py:34
  406.9 6.5 %collective-permute-start.65 = (f32[8,6,1,32]{0,3,2,1:T(8,128)S(1)}, f32[8,6,1,32]{0,3,2,1:T(8,128)S(1)}, u32[]{:S(2)}, u32[]{:S(2)}) collective-permute-start(f32[8,6,1,32]{0,3,2,1:T(8,128)S(1)} %get-tuple-element.61), channel_id=1, source_target_pairs={{1,0},{2,1},{3,2},{5,4},{6,5},{7,6},{9,8},{10,9},{11,10},{13,12},{... | collective-permute-start | bytes 18440 | tf_op jit(solution)/shard_map/ppermute | solution.py:36
  (130 other events, 1956.1 us)
